TPU v7x, 32 devices: a whole 2x2x4 slice. The times are simulated.
32 devices in a mesh: seg: 4 (over y, core), tile: 8 (over z, x).
Axes of the slice: x: 2, y: 2, z: 4, core: 2. Of those that a mesh axis runs over, the one named last changes fastest.
Arguments:
- raw: bfloat16 [8192, 12288], P('tile', 'seg'), may hold values from -6 to 6
- filters: bfloat16 [32, 128], replicated, may hold values from -0.5 to 0.5
- weights: bfloat16 [8, 32, 4096, 128], P('tile', 'seg'), may hold values from -0.09375 to 0.09375
- blocks: int32 [8, 32], replicated, may hold values from 0 to 95, as said below
- shifts: int32 [8, 32], replicated, may hold values from 0 to 64
Outputs:
- image: bfloat16 [8, 16, 64, 4096], P('tile', None, None, 'seg')
Inputs may be any that keep to these rules, and one draw needn't show every extreme that they name: Block numbers of the record's 128-channel blocks. Take any s and t, and the entries s * 8 to (s + 1) * 8 - 1 of the tiles t * 1 to (t + 1) - 1: at most 3 of them name blocks of one fibre segment (blocks k * 24 to (k + 1) * 24 - 1), and some segment is named by exactly 3 of them. A block may stand more than once in a tile's list.
All inputs are finite; a program needn't handle non-finite values.
Results may differ from a plain program's by a relative error of at most 0.0049.
Values may be sent and summed in bfloat16 or wider, within the bound.
A program may use at most 128 MiB of HBM per device.

v0:
```python
import jax
import jax.numpy as jnp
from jax import lax
from jax.sharding import PartitionSpec as P

MAXSHIFT = 64
CAP = 3


def from_behind(block, axis, distance):
    devices = range(lax.axis_size(axis))
    route = [(i - distance, i) for i in devices if i - distance in devices]
    return lax.ppermute(block, axis, route)


def cut_windows(series_all, delay_all, steps_out):
    return jax.vmap(lambda series, delay: lax.dynamic_slice_in_dim(series, delay, steps_out, 1))(
        series_all, delay_all
    )


def local(raw, filters, weights, blocks, shifts):
    seg_count = lax.axis_size("seg")
    tile_count = lax.axis_size("tile")
    seg_index = lax.axis_index("seg")
    tile_index = lax.axis_index("tile")
    samples, channels = raw.shape
    hop_length = filters.shape[1] // 2
    filter_count = filters.shape[0] // 2
    block_width = weights.shape[3]
    per_seg = channels // block_width
    frames_dev = samples // hop_length
    tile_dev = weights.shape[0]
    entries_dev = weights.shape[1]
    slot_count = tile_dev * entries_dev
    next_rim = from_behind(raw[:hop_length], "tile", -1)
    extended = jnp.concatenate([raw, next_rim], 0)
    hop_frame_rows = extended.reshape(frames_dev + 1, hop_length, channels)
    filter_bank_output = jnp.einsum(
        "xt,stm->xsm",
        filters[:, :hop_length],
        hop_frame_rows[:-1],
        preferred_element_type=jnp.float32,
    )
    filter_bank_output = filter_bank_output + jnp.einsum(
        "xt,stm->xsm",
        filters[:, hop_length:],
        hop_frame_rows[1:],
        preferred_element_type=jnp.float32,
    )
    signal_envelope = jnp.sqrt(
        filter_bank_output[:filter_count] ** 2 + filter_bank_output[filter_count:] ** 2
    ).astype(jnp.bfloat16)
    pieces = signal_envelope.reshape(filter_count, frames_dev, per_seg, block_width).transpose(
        2, 0, 1, 3
    )
    grouped = (
        blocks.reshape(tile_count, tile_dev, seg_count, entries_dev)
        .transpose(2, 0, 1, 3)
        .reshape(seg_count, tile_count, slot_count)
    )
    delays = (
        shifts.reshape(tile_count, tile_dev, seg_count, entries_dev)
        .transpose(2, 0, 1, 3)
        .reshape(seg_count, tile_count, slot_count)
    )
    source_seg = grouped // per_seg
    same_seg = source_seg[..., :, None] == source_seg[..., None, :]
    before = lax.broadcasted_iota(jnp.int32, (slot_count, slot_count), 1) < lax.broadcasted_iota(
        jnp.int32, (slot_count, slot_count), 0
    )
    slot_rank = jnp.sum(jnp.where(same_seg & before, 1, 0), -1).astype(jnp.int32)
    own_seg = source_seg[seg_index, tile_index]
    own_rank = slot_rank[seg_index, tile_index]
    own_delay = delays[seg_index, tile_index]
    cap_slots = jnp.arange(CAP, dtype=jnp.int32)
    matches = (source_seg[..., None, :] == seg_index) & (
        slot_rank[..., None, :] == cap_slots[:, None]
    )
    chosen = jnp.where(matches, grouped[..., None, :] - seg_index * per_seg, 0)
    local_ids = jnp.sum(chosen, -1)
    outgoing = jnp.take(pieces, local_ids.reshape(-1), axis=0).reshape(
        seg_count * tile_count, CAP, filter_count, frames_dev, block_width
    )
    received = lax.all_to_all(outgoing, ("seg", "tile"), split_axis=0, concat_axis=0, tiled=True)
    received = received.reshape(seg_count, tile_count, CAP, filter_count, frames_dev, block_width)
    full_time = (
        received[own_seg, :, own_rank]
        .transpose(0, 2, 1, 3, 4)
        .reshape(slot_count, filter_count, tile_count * frames_dev, block_width)
    )
    windows = cut_windows(full_time, own_delay, full_time.shape[2] - MAXSHIFT)
    steps_out = windows.shape[2]
    windows = windows.reshape(tile_dev, entries_dev, filter_count, steps_out, block_width)
    partial_value = jnp.einsum(
        "mepc,meftc->mftp", weights, windows, preferred_element_type=jnp.float32
    )
    return lax.psum_scatter(partial_value, "seg", scatter_dimension=3, tiled=True).astype(
        jnp.bfloat16
    )


def solution(mesh):
    return jax.shard_map(
        local,
        mesh=mesh,
        in_specs=(P("tile", "seg"), P(), P("tile", "seg", None, None), P(), P()),
        out_specs=P("tile", None, None, "seg"),
        check_vma=False,
    )
```

profile of v0, /device:TPU:16, one launch (start us, length us, event | category | flops | bytes accessed | tf_op | source)
XLA Modules:
  0.0 358.6 jit_solution(12308912241601751638)
XLA Ops:
  6.5 1.8 slice.27
  8.3 3.3 collective-permute-start
  11.6 0.7 fusion.12
  12.4 0.7 broadcast_divide_fusion
  13.3 0.7 select_reduce_fusion
  14.5 0.7 copy.35
  15.3 0.6 pad_clamp_fusion
  15.9 6.6 %fusion.8 = f32[32,16,3072]{2,0,1:T(8,128)} fusion(bf16[16,64,3072]{2,1,0:T(8,128)(2,1)} %bitcast.86, bf16[32,128]{1,0:T(8,128)(2,1)} %param.6), kind=kOutput, calls=%fused_computation.24 | convolution fusion | flops 201326592 | bytes 12591104 | tf_op jit(solution)/shard_map/xt,stm->xsm/dot_general | solution.py:39
  22.5 3.1 pad_maximum_fusion
  25.6 5.7 %bitcast_add_fusion = f32[32,16,3072]{2,0,1:T(8,128)S(1)} fusion(f32[32,16,3072]{2,0,1:T(8,128)} %fusion.8, bf16[16,64,3072]{2,1,0:T(8,128)(2,1)} %bitcast.90, bf16[32,128]{1,0:T(8,128)(2,1)S(1)} %copy-done), kind=kOutput, calls=%fused_computation.6 | convolution fusion | flops 202899456 | bytes 18882560 | tf_op jit(solution)/shard_map/xt,stm->xsm/dot_general | solution.py:45
  31.3 1.1 fusion.3
  32.4 0.3 copy.43
  32.7 1.0 copy.59
  33.7 6.1 %gather_fusion = bf16[96,16,16,128]{3,2,1,0:T(8,128)(2,1)} fusion(bf16[24,16,16,128]{3,2,1,0:T(8,128)(2,1)S(1)} %bitcast.85, s32[1024]{0:T(1024)} %pad_clamp_fusion), kind=kCustom, calls=%fused_computation | custom fusion | bytes 12583296 | tf_op jit(solution)/shard_map/jit(_take)/gather | solution.py:82
  39.8 6.1 %broadcast_select_fusion = bf16[32,3,16,16,128]{4,3,2,1,0:T(8,128)(2,1)} fusion(bf16[32,3,16,16,128]{4,3,2,1,0:T(8,128)(2,1)} %bitcast.89, pred[32,3]{1,0:T(8,128)(4,1)S(1)} %copy-done.1), kind=kLoop, calls=%fused_computation.7 | loop fusion | flops 3145728 | bytes 12583008 | tf_op jit(solution)/shard_map/jit(_take)/select_n | solution.py:82
  45.9 5.1 %all-to-all-start = ((bf16[32,3,16,16,128]{4,3,2,1,0:T(8,128)(2,1)}), bf16[32,3,16,16,128]{4,3,2,1,0:T(8,128)(2,1)}, u32[]{:S(2)}, u32[]{:S(2)}) async-start(bf16[32,3,16,16,128]{4,3,2,1,0:T(8,128)(2,1)} %broadcast_select_fusion), calls=%async_computation | async-start | bytes 12582912 | tf_op jit(solution)/shard_map/all_to_all | solution.py:85
  51.4 137.2 %all-to-all-done = bf16[32,3,16,16,128]{4,3,2,1,0:T(8,128)(2,1)} async-done(((bf16[32,3,16,16,128]{4,3,2,1,0:T(8,128)(2,1)}), bf16[32,3,16,16,128]{4,3,2,1,0:T(8,128)(2,1)}, u32[]{:S(2)}, u32[]{:S(2)}) %all-to-all-start) | async-done | bytes 6291488 | tf_op jit(solution)/shard_map/all_to_all | solution.py:85
  188.6 5.9 %gather_fusion.1 = bf16[8,8,16,16,128]{4,3,2,1,0:T(8,128)(2,1)} fusion(bf16[4,8,3,16,16,128]{5,4,3,2,1,0:T(8,128)(2,1)} %bitcast.16, s32[8]{0:T(128)S(1)} %or_bitcast_fusion.1), kind=kCustom, calls=%fused_computation.1 | custom fusion | bytes 8388672 | tf_op jit(solution)/shard_map/gather | solution.py:88
  194.5 3.4 copy.38
  197.9 4.6 %copy.40 = bf16[8,16,128,128]{3,1,0,2:T(8,128)(2,1)} copy(bf16[8,16,128,128]{3,2,1,0:T(8,128)(2,1)S(1)} %bitcast.91) | data formatting | bytes 8388608 | tf_op jit(solution)/shard_map/reshape | solution.py:90
  202.5 3.3 gather_fusion.2
  205.8 14.5 %convolution_bitcast_fusion = f32[1,16,64,4096]{3,2,1,0:T(8,128)} fusion(bf16[1,8,4096,128]{3,2,1,0:T(8,128)(2,1)} %param.7, bf16[8,16,64,128]{3,1,2,0:T(8,128)(2,1)S(1)} %gather_fusion.2), kind=kOutput, calls=%fused_computation.3 | convolution fusion | flops 8589934592 | bytes 27262976 | tf_op jit(solution)/shard_map/mepc,meftc->mftp/dot_general | solution.py:95
  220.3 127.6 %reduce-scatter.2.cloned.1.call-done = f32[1,16,64,1024]{3,2,1,0:T(8,128)} async-done(((f32[1,16,64,4096]{3,2,1,0:T(8,128)}), f32[1,16,64,1024]{3,2,1,0:T(8,128)}) %reduce-scatter.2.cloned.1.call-update) | async-done | bytes 4194320 | tf_op jit(solution)/shard_map/reduce_scatter | solution.py:98
  347.9 3.8 %convert_element_type.7 = bf16[1,16,64,1024]{3,2,1,0:T(8,128)(2,1)} convert(f32[1,16,64,1024]{3,2,1,0:T(8,128)} %reduce-scatter.2.cloned.1.call-done) | non-fusion elementwise | flops 1048576 | bytes 6291456 | tf_op jit(solution)/shard_map/convert_element_type | solution.py:98
  (32 shorter events, 1.2 us)
Async XLA Ops:
  8.3 14.2 %collective-permute-start = (bf16[64,3072]{1,0:T(8,128)(2,1)}, bf16[64,3072]{1,0:T(8,128)(2,1)S(1)}, u32[]{:S(2)}, u32[]{:S(2)}) collective-permute-start(bf16[64,3072]{1,0:T(8,128)(2,1)} %slice.27), channel_id=1, source_target_pairs={{1,0},{2,1},{3,2},{4,3},{5,4},{6,5},{7,6},{9,8},{10,9},{11,10},{12... | collective-permute-start | bytes 1179656 | tf_op jit(solution)/shard_map/ppermute | solution.py:13
  13.3 9.2 %slice-start = ((s8[6291456]{0:T(1024)(128)(4,1)}), s8[2097152]{0:T(1024)(128)(4,1)S(1)}, s32[]{:S(2)}) async-start(s8[6291456]{0:T(1024)(128)(4,1)} %bitcast.87), calls=%async_computation.3 | async-start | bytes 4194304
  15.9 6.6 %slice-start.1 = ((s8[6291456]{0:T(1024)(128)(4,1)}), s8[4194304]{0:T(1024)(128)(4,1)S(1)}, s32[]{:S(2)}) async-start(s8[6291456]{0:T(1024)(128)(4,1)} %bitcast.87), calls=%async_computation.4 | async-start | bytes 8388608
  22.5 3.1 copy-start
  33.7 6.1 %copy-start.1 = (pred[32,3]{1,0:T(8,128)(4,1)S(1)}, pred[32,3]{1,0:T(8,128)(4,1)}, u32[]{:S(2)}) copy-start(pred[32,3]{1,0:T(8,128)(4,1)} %copy.35) | copy-start | bytes 292
  45.9 5.4 %copy-start.2 = (s32[8,32]{1,0:T(8,128)S(1)}, s32[8,32]{1,0:T(8,128)}, u32[]{:S(2)}) copy-start(s32[8,32]{1,0:T(8,128)} %param.9) | copy-start | bytes 3076
  45.9 142.7 %all-to-all-start = ((bf16[32,3,16,16,128]{4,3,2,1,0:T(8,128)(2,1)}), bf16[32,3,16,16,128]{4,3,2,1,0:T(8,128)(2,1)}, u32[]{:S(2)}, u32[]{:S(2)}) async-start(bf16[32,3,16,16,128]{4,3,2,1,0:T(8,128)(2,1)} %broadcast_select_fusion), calls=%async_computation | async-start | bytes 12582912 | tf_op jit(solution)/shard_map/all_to_all | solution.py:85
  51.0 296.9 %reduce-scatter.2.cloned.1.call-start = ((), (), s32[]{:S(2)}) async-start(), calls=%async_computation.2 | async-start | bytes 20971520 | tf_op jit(solution)/shard_map/reduce_scatter | solution.py:98
Sparse Core Ops, SparseCore 0:
  220.4 127.4 reduce-scatter.1
where the time goes:
time: 361 us; the launch traced here: 359 us
  waiting for transfers between devices  265 us (73%)
  local copies, waits for them, and re-layouts  27.7 us (8%)
  matrix products  26.7 us (7%)
  other arithmetic  17.1 us (5%)
  between operations  13.6 us (4%)
  starting transfers between devices  8.64 us (2%)
    all_to_all x1, waiting for transfers between devices, local(): lax.all_to_all(outgoing, ('seg', 'tile'), split_axis=0, concat_axis=0, ti...  137 us
    reduce_scatter x1, waiting for transfers between devices, local(): lax.psum_scatter(partial_value, 'seg', scatter_dimension=3, tiled=True)  128 us
    dot_general x1, matrix products, local(): jnp.einsum('mepc,meftc->mftp', weights, windows, preferred_element_type=j...  14.5 us
  transfers between devices with their start and end apart: 3, of which 2 were waited for; matrix products, arithmetic and copies ran while one was open for 3% of the time, Pallas kernels for 0%

commit v1 on v0

v1 whole, which is shorter than its diff:
```python
import functools

import jax
import jax.numpy as jnp
from jax import lax
from jax.experimental import pallas as pl
from jax.experimental.pallas import tpu as pltpu
from jax.sharding import PartitionSpec as P

MAXSHIFT = 64
CHUNKS = 4
CORES = 2


def kernel(
    dims,
    raw_ref,
    taps_ref,
    weights_ref,
    blocks_ref,
    shifts_ref,
    out_ref,
    raw_x,
    w_all,
    onehot,
    lhs,
    picked,
    landed,
    near_s,
    near_r,
    far_s,
    far_r,
    own_s,
    own_r,
    own_f,
    mine_f,
    *rest,
):
    seg_count, tile_count, hop, frames, per_seg, entries, steps, fc = dims
    gathered = rest[:CHUNKS]
    (raw_sem, w_sem, halo_sem, g_send, g_recv, a_send, a_recv, a_loc, r_send, r_recv) = rest[CHUNKS:]
    rows = fc * frames
    out_rows = fc * steps
    samples = raw_ref.shape[0]
    part = out_ref.shape[1]
    rings = seg_count // CORES
    s = lax.axis_index("seg")
    t = lax.axis_index("tile")
    core = lax.rem(s, CORES)
    y = s // CORES
    mate = s + 1 - 2 * core

    def peer_y(dy):
        return lax.rem(y + dy, rings) * CORES + core

    def peer_t(dt):
        return lax.rem(t + dt, tile_count)

    raw_copy = pltpu.make_async_copy(raw_ref, raw_x.at[pl.ds(0, samples)], raw_sem.at[0])
    raw_copy.start()

    barrier = pltpu.get_barrier_semaphore()
    pl.semaphore_signal(barrier, inc=1, device_id={"seg": mate}, device_id_type=pl.DeviceIdType.MESH)
    for dy in range(1, rings):
        pl.semaphore_signal(
            barrier, inc=1, device_id={"seg": peer_y(dy)}, device_id_type=pl.DeviceIdType.MESH
        )
    for dt in range(1, tile_count):
        pl.semaphore_signal(
            barrier, inc=1, device_id={"tile": peer_t(dt)}, device_id_type=pl.DeviceIdType.MESH
        )
    pl.semaphore_wait(barrier, 1 + rings - 1 + tile_count - 1)

    def remote(src, dst, send, recv, **device):
        return pltpu.make_async_remote_copy(
            src_ref=src,
            dst_ref=dst,
            send_sem=send,
            recv_sem=recv,
            device_id=device,
            device_id_type=pl.DeviceIdType.MESH,
        )

    rim = pl.ds(samples, hop)
    halo = remote(
        raw_ref.at[pl.ds(0, hop)],
        raw_x.at[rim],
        halo_sem.at[0],
        halo_sem.at[1],
        tile=lax.rem(t + tile_count - 1, tile_count),
    )

    @pl.when(t > 0)
    def _():
        halo.start()

    w_copies = []
    for e in range(entries):
        copy = pltpu.make_async_copy(
            weights_ref.at[0, e], w_all.at[:, pl.ds(e * 128, 128)], w_sem.at[e]
        )
        copy.start()
        w_copies.append(copy)

    raw_copy.wait()

    @pl.when(t < tile_count - 1)
    def _():
        halo.wait_recv()

    @pl.when(t == tile_count - 1)
    def _():
        raw_x[rim, :] = jnp.zeros((hop, raw_x.shape[1]), raw_x.dtype)

    pending = []
    wide = 2 if per_seg % 2 == 0 else 1

    def own_slots(seg):
        return pl.ds(seg * per_seg, per_seg)

    def envelope(k):
        grid = gathered[k]

        def body(i, carry):
            cols = pl.ds(pl.multiple_of(i * (wide * 128), wide * 128), wide * 128)
            both = jnp.dot(taps_ref[k], raw_x[:, cols], preferred_element_type=jnp.float32)
            inphase, quadrature = both[:rows], both[rows:]
            env = jnp.sqrt(inphase * inphase + quadrature * quadrature).astype(jnp.bfloat16)
            for b in range(wide):
                grid[s * per_seg + i * wide + b] = env[:, b * 128 : (b + 1) * 128]
            return carry

        lax.fori_loop(0, per_seg // wide, body, 0)
        held = grid.at[own_slots(s)]
        copies = []
        for dy in range(1, rings):
            copies.append(remote(held, held, g_send.at[k, dy], g_recv.at[k, dy], seg=peer_y(dy)))
        copies.append(remote(held, held, g_send.at[k, 0], g_recv.at[k, 0], seg=mate))
        for copy in copies:
            copy.start()
        pending.extend(copies)
        return copies

    def exchange(k, copies):
        grid = gathered[k]
        forwards = []
        for dy in range(1, rings):
            copies[dy - 1].wait_recv()
            origin = lax.rem(y + rings - dy, rings) * CORES + core
            held = grid.at[own_slots(origin)]
            copy = remote(
                held, held, g_send.at[k, rings + dy - 1], g_recv.at[k, rings + dy - 1], seg=mate
            )
            copy.start()
            forwards.append(copy)
        copies[-1].wait_recv()
        for copy in forwards:
            copy.wait_recv()
        pending.extend(forwards)

        def pick(j, carry):
            for e in range(entries):
                picked[k, j, e] = grid[blocks_ref[j, s * entries + e]]
            return carry

        lax.fori_loop(0, tile_count, pick, 0)
        sent = []
        order = sorted(range(1, tile_count), key=lambda dt: -min(dt, tile_count - dt))
        for dt in order:
            copy = remote(
                picked.at[k, peer_t(dt)],
                landed.at[k, t],
                a_send.at[k, dt],
                a_recv.at[k, dt],
                tile=peer_t(dt),
            )
            copy.start()
            sent.append(copy)
        local = pltpu.make_async_copy(picked.at[k, t], landed.at[k, t], a_loc.at[k])
        local.start()
        pending.extend(sent)
        return sent, local

    def make_onehot():
        shape = (out_rows, tile_count * rows)
        m = lax.broadcasted_iota(jnp.int32, shape, 0)
        n = lax.broadcasted_iota(jnp.int32, shape, 1)
        frame = (n // rows) * frames + n % frames
        gap = jnp.where(m // steps == (n // frames) % fc, frame - m % steps, -1)

        def body(e, carry):
            d = shifts_ref[t, s * entries + e]
            onehot[e] = jnp.where(gap == d, 1.0, 0.0).astype(jnp.bfloat16)
            return carry

        lax.fori_loop(0, entries, body, 0)

    tile_p = min(256, part)

    def multiply(q, store):
        def body(i, carry):
            start = pl.multiple_of(i * tile_p, tile_p)
            value = lax.dot_general(
                lhs[...],
                w_all[pl.ds(pl.multiple_of(q * part + start, tile_p), tile_p), :],
                (((1,), (1,)), ((), ())),
                preferred_element_type=jnp.float32,
            )
            store(pl.ds(start, tile_p), value)
            return carry

        lax.fori_loop(0, part // tile_p, body, 0)

    def stack(k, arrivals):
        sent, local = arrivals
        for copy in sent:
            copy.wait_recv()
        local.wait()

        def shift(e, carry):
            series = landed[k, :, e].reshape(tile_count * rows, 128)
            lanes = pl.ds(pl.multiple_of(e * 128, 128), 128)
            lhs[:, lanes] = jnp.dot(
                onehot[e], series, preferred_element_type=jnp.float32
            ).astype(jnp.bfloat16)
            return carry

        lax.fori_loop(0, entries, shift, 0)
        if k == 0:
            for copy in w_copies:
                copy.wait()
        far = []
        for dy in range(1, rings):
            yy = lax.rem(y + dy, rings)
            i = dy - 1

            def put_near(cols, value):
                near_s[k, i, :, cols] = value.astype(jnp.bfloat16)

            multiply(yy * CORES + 1 - core, put_near)
            near = remote(near_s.at[k, i], near_r.at[k, i], r_send.at[k, i], r_recv.at[k, i], seg=mate)
            near.start()

            def put_mine(cols, value):
                mine_f[:, cols] = value

            multiply(yy * CORES + core, put_mine)
            near.wait_recv()
            far_s[k, i] = (mine_f[...] + near_r[k, i].astype(jnp.float32)).astype(jnp.bfloat16)
            copy = remote(
                far_s.at[k, i],
                far_r.at[k, i],
                r_send.at[k, rings - 1 + i],
                r_recv.at[k, rings - 1 + i],
                seg=peer_y(dy),
            )
            copy.start()
            far.append(copy)
            pending.append(near)

        def put_own(cols, value):
            own_s[k, :, cols] = value.astype(jnp.bfloat16)

        multiply(y * CORES + 1 - core, put_own)
        own = remote(
            own_s.at[k], own_r.at[k], r_send.at[k, 2 * rings - 2], r_recv.at[k, 2 * rings - 2], seg=mate
        )
        own.start()

        def keep(cols, value):
            own_f[k, :, cols] = value

        multiply(s, keep)
        pending.extend(far)
        pending.append(own)
        return far, own

    def finish(k, sums):
        far, own = sums
        own.wait_recv()
        total = own_f[k] + own_r[k].astype(jnp.float32)
        for i, copy in enumerate(far):
            copy.wait_recv()
            total = total + far_r[k, i].astype(jnp.float32)
        out_ref[pl.ds(k * out_rows, out_rows), :] = total.astype(jnp.bfloat16)

    gathers = {}
    arrivals = {}
    gathers[0] = envelope(0)
    for k in range(CHUNKS):
        if k + 1 < CHUNKS:
            gathers[k + 1] = envelope(k + 1)
        arrivals[k] = exchange(k, gathers[k])
    make_onehot()
    sums = {}
    for k in range(CHUNKS):
        sums[k] = stack(k, arrivals[k])
        if k:
            finish(k - 1, sums[k - 1])
    finish(CHUNKS - 1, sums[CHUNKS - 1])

    for copy in pending:
        copy.wait_send()

    @pl.when(t > 0)
    def _():
        halo.wait_send()


def local(raw, filters, weights, blocks, shifts):
    seg_count = lax.axis_size("seg")
    tile_count = lax.axis_size("tile")
    samples, channels = raw.shape
    taps = filters.shape[1]
    hop = taps // 2
    bank = filters.shape[0] // 2
    per_seg = channels // weights.shape[3]
    frames = samples // hop
    entries = weights.shape[1]
    points = weights.shape[2]
    part = points // seg_count
    steps = tile_count * frames - MAXSHIFT
    fc = bank // CHUNKS
    rows = fc * frames
    out_rows = fc * steps
    rings = seg_count // CORES
    depth = samples + hop
    bf16 = jnp.bfloat16
    banded = jnp.stack(
        [
            jnp.pad(filters, ((0, 0), (hop * i, depth - taps - hop * i)))
            for i in range(frames)
        ],
        1,
    )
    banded = (
        banded.reshape(2, CHUNKS, fc, frames, depth)
        .transpose(1, 0, 2, 3, 4)
        .reshape(CHUNKS, 2 * rows, depth)
    )
    dims = (seg_count, tile_count, hop, frames, per_seg, entries, steps, fc)
    other = max(rings - 1, 1)
    image = pl.pallas_call(
        functools.partial(kernel, dims),
        out_shape=jax.ShapeDtypeStruct((CHUNKS * out_rows, part), bf16),
        in_specs=[
            pl.BlockSpec(memory_space=pl.ANY),
            pl.BlockSpec(memory_space=pltpu.VMEM),
            pl.BlockSpec(memory_space=pl.ANY),
            pl.BlockSpec(memory_space=pltpu.SMEM),
            pl.BlockSpec(memory_space=pltpu.SMEM),
        ],
        out_specs=pl.BlockSpec(memory_space=pltpu.VMEM),
        scratch_shapes=[
            pltpu.VMEM((depth, channels), bf16),
            pltpu.VMEM((points, entries * 128), bf16),
            pltpu.VMEM((entries, out_rows, tile_count * rows), bf16),
            pltpu.VMEM((out_rows, entries * 128), bf16),
            pltpu.VMEM((CHUNKS, tile_count, entries, rows, 128), bf16),
            pltpu.VMEM((CHUNKS, tile_count, entries, rows, 128), bf16),
            pltpu.VMEM((CHUNKS, other, out_rows, part), bf16),
            pltpu.VMEM((CHUNKS, other, out_rows, part), bf16),
            pltpu.VMEM((CHUNKS, other, out_rows, part), bf16),
            pltpu.VMEM((CHUNKS, other, out_rows, part), bf16),
            pltpu.VMEM((CHUNKS, out_rows, part), bf16),
            pltpu.VMEM((CHUNKS, out_rows, part), bf16),
            pltpu.VMEM((CHUNKS, out_rows, part), jnp.float32),
            pltpu.VMEM((out_rows, part), jnp.float32),
            *[pltpu.VMEM((seg_count * per_seg, rows, 128), bf16) for _ in range(CHUNKS)],
            pltpu.SemaphoreType.DMA((1,)),
            pltpu.SemaphoreType.DMA((entries,)),
            pltpu.SemaphoreType.DMA((2,)),
            pltpu.SemaphoreType.DMA((CHUNKS, 2 * rings)),
            pltpu.SemaphoreType.DMA((CHUNKS, 2 * rings)),
            pltpu.SemaphoreType.DMA((CHUNKS, tile_count)),
            pltpu.SemaphoreType.DMA((CHUNKS, tile_count)),
            pltpu.SemaphoreType.DMA((CHUNKS,)),
            pltpu.SemaphoreType.DMA((CHUNKS, 2 * rings)),
            pltpu.SemaphoreType.DMA((CHUNKS, 2 * rings)),
        ],
        compiler_params=pltpu.CompilerParams(
            collective_id=0, has_side_effects=True, vmem_limit_bytes=60 * 1024 * 1024
        ),
    )(raw, banded, weights, blocks, shifts)
    return image.reshape(1, bank, steps, part)


def solution(mesh):
    return jax.shard_map(
        local,
        mesh=mesh,
        in_specs=(P("tile", "seg"), P(), P("tile", "seg", None, None), P(), P()),
        out_specs=P("tile", None, None, "seg"),
        check_vma=False,
    )
```

time: 361 us -> 158 us (0.44)
  waiting for transfers between devices: 265 us -> 0 us
  Pallas kernels: 0 us -> 143 us
  matrix products: 26.7 us -> 0 us
  other arithmetic: 17.1 us -> 0 us
  local copies, waits for them, and re-layouts: 27.7 us -> 13.9 us
  between operations: 13.6 us -> 0.21 us
  starting transfers between devices: 8.64 us -> 0 us
    pallas_call x0 -> x1, Pallas kernels: none -> 143 us  [local(): pl.pallas_call(functools.partial(kernel, dims), out_shape=jax.ShapeDtypeS...]
    all_to_all x1 -> x0, waiting for transfers between devices: 137 us -> none  [local(): lax.all_to_all(outgoing, ('seg', 'tile'), split_axis=0, concat_axis=0, ti...]
    reduce_scatter x1 -> x0, waiting for transfers between devices: 128 us -> none  [local(): lax.psum_scatter(partial_value, 'seg', scatter_dimension=3, tiled=True)]
    dot_general x3 -> x0, matrix products: 26.7 us -> none  [the longest x1 14.5 us: local(): jnp.einsum('mepc,meftc->mftp', weights, windows, preferred_element_type=j...]
    gather x3 -> x0, local copies, waits for them, and re-layouts: 15.3 us -> none  [the longest x1 6.11 us: local(): jnp.take(pieces, local_ids.reshape(-1), axis=0)]
    another operation x0 -> x33, local copies, waits for them, and re-layouts: none -> 9.58 us  [local(): jnp.stack([jnp.pad(filters, ((0, 0), (hop * i, depth - taps - hop * i)))...]
    select_n x3 -> x0, other arithmetic: 6.07 us -> none  [the longest x2 6.06 us: local(): jnp.take(pieces, local_ids.reshape(-1), axis=0)]
    reshape x5 -> x0, local copies, waits for them, and re-layouts: 5.91 us -> none  [the longest x1 4.64 us: local(): full_time = received[own_seg, :, own_rank].transpose(0, 2, 1, 3, 4).resha...]
  transfers between devices with their start and end apart: 3 -> 0, of which waited for: 2 -> 0; matrix products, arithmetic and copies ran while one was open for 3% -> 0% of each run, Pallas kernels for 0% -> 0%
where the time goes in v1:
time: 158 us; the launch traced here: 157 us
  Pallas kernels  143 us (91%)
  local copies, waits for them, and re-layouts  13.9 us (9%)
    pallas_call x1, Pallas kernels, local(): pl.pallas_call(functools.partial(kernel, dims), out_shape=jax.ShapeDtypeS...  143 us
    another operation x33, local copies, waits for them, and re-layouts, local(): jnp.stack([jnp.pad(filters, ((0, 0), (hop * i, depth - taps - hop * i)))...  9.58 us

profile of v1, /device:TPU:16, one launch (start us, length us, event | category | flops | bytes accessed | tf_op | source)
XLA Modules:
  0.0 157.3 jit_solution(12317457764791578333)
XLA Ops:
  0.0 0.0 copy-start
  0.0 1.1 fusion.1
  1.1 0.1 copy.20
  1.3 0.1 copy.11
  1.4 0.1 copy.10
  1.6 0.1 copy.9
  1.7 0.1 copy.8
  1.9 0.1 copy.7
  2.0 0.1 copy.6
  2.1 0.0 copy-done
  2.1 0.1 fusion
  2.3 0.1 copy.21
  2.4 0.1 copy.19
  2.6 0.1 copy.18
  2.7 0.1 copy.17
  2.9 0.1 copy.16
  3.0 0.1 copy.15
  3.2 0.1 copy.14
  3.3 0.1 copy.13
  3.5 0.1 copy.12
  3.6 7.3 %stack.67 = bf16[2,4,4,16,1088]{4,3,2,0,1:T(8,128)(2,1)} concatenate(bf16[2,4,4,1,1088]{4,3,2,0,1:T(2,128)(2,1)S(1)} %copy.6, bf16[2,4,4,1,1088]{4,3,2,0,1:T(2,128)(2,1)S(1)} %copy.7, bf16[2,4,4,1,1088]{4,3,2,0,1:T(2,128)(2,1)S(1)} %copy.8, bf16[2,4,4,1,1088]{4,3,2,0,1:T(2,128)(2,1)S(1)} %copy.9, bf16[2,4,4,1,1088]{4,3,2,0,1:T(2,128)(2,1)S(1)} %copy.10, ...), dimensions={3} | concatenate | bytes 2228224 | tf_op jit(solution)/shard_map/stack | solution.py:329
  10.9 143.2 %shard_map.55 = bf16[1024,1024]{1,0:T(8,128)(2,1)} custom-call(bf16[1024,3072]{1,0:T(8,128)(2,1)} %raw_ref.1, bf16[4,128,1088]{2,1,0:T(8,128)(2,1)} %bitcast.5, bf16[1,8,4096,128]{3,2,1,0:T(8,128)(2,1)} %weights_ref.1, s32[8,32]{1,0:T(8,128)} %blocks_ref.1, s32[8,32]{1,0:T(8,128)} %shifts_ref.1), custom_call_target="tpu_custom_call" | custom-call | tf_op jit(solution)/shard_map/pallas_call | solution.py:343
  154.2 3.1 %copy.23 = bf16[1,16,64,1024]{3,2,1,0:T(8,128)(2,1)} copy(bf16[1,16,64,1024]{3,2,1,0:T(8,128)(2,1)} %bitcast.4) | data formatting | bytes 4194304
  (16 shorter events, 0.4 us)
Async XLA Ops:
  0.0 2.1 %copy-start = (bf16[32,128]{1,0:T(8,128)(2,1)S(1)}, bf16[32,128]{1,0:T(8,128)(2,1)}, u32[]{:S(2)}) copy-start(bf16[32,128]{1,0:T(8,128)(2,1)} %param.6) | copy-start | bytes 24580

commit v2 on v1

--- a/solution.py
+++ b/solution.py
@@ -8,7 +8,7 @@
 from jax.sharding import PartitionSpec as P
 
 MAXSHIFT = 64
-CHUNKS = 4
+CHUNKS = 8
 CORES = 2
 
 
@@ -34,6 +34,7 @@
     own_r,
     own_f,
     mine_f,
+    band,
     *rest,
 ):
     seg_count, tile_count, hop, frames, per_seg, entries, steps, fc = dims
@@ -102,34 +103,43 @@
         copy.start()
         w_copies.append(copy)
 
-    raw_copy.wait()
-
-    @pl.when(t < tile_count - 1)
-    def _():
-        halo.wait_recv()
-
-    @pl.when(t == tile_count - 1)
-    def _():
-        raw_x[rim, :] = jnp.zeros((hop, raw_x.shape[1]), raw_x.dtype)
-
     pending = []
     wide = 2 if per_seg % 2 == 0 else 1
 
     def own_slots(seg):
         return pl.ds(seg * per_seg, per_seg)
 
+    def make_band(k):
+        bank = taps_ref.shape[0]
+        row = lax.broadcasted_iota(jnp.int32, (2 * rows, bank), 0)
+        col = lax.broadcasted_iota(jnp.int32, (2 * rows, bank), 1)
+        wanted = (row // rows) * (bank // 2) + k * fc + (row // frames) % fc
+        pick_rows = jnp.where(wanted == col, 1.0, 0.0).astype(jnp.bfloat16)
+        taps = jnp.dot(pick_rows, taps_ref[...], preferred_element_type=jnp.float32)
+        turned = jnp.concatenate([taps[:, hop:], taps[:, :hop]], 1)
+        frame = lax.broadcasted_iota(jnp.int32, taps.shape, 0) % frames
+        lane = lax.broadcasted_iota(jnp.int32, taps.shape, 1)
+        for m in range((samples + hop + 2 * hop - 1) // (2 * hop)):
+            left = m * 2 * hop
+            width = min(2 * hop, samples + hop - left)
+            odd = frame == jnp.where(lane < hop, 2 * m - 1, 2 * m + 1)
+            value = jnp.where(frame == 2 * m, taps, jnp.where(odd, turned, 0.0))
+            band[:, left : left + width] = value[:, :width].astype(jnp.bfloat16)
+
     def envelope(k):
         grid = gathered[k]
 
         def body(i, carry):
             cols = pl.ds(pl.multiple_of(i * (wide * 128), wide * 128), wide * 128)
-            both = jnp.dot(taps_ref[k], raw_x[:, cols], preferred_element_type=jnp.float32)
+            both = jnp.dot(band[...], raw_x[:, cols], preferred_element_type=jnp.float32)
             inphase, quadrature = both[:rows], both[rows:]
             env = jnp.sqrt(inphase * inphase + quadrature * quadrature).astype(jnp.bfloat16)
             for b in range(wide):
                 grid[s * per_seg + i * wide + b] = env[:, b * 128 : (b + 1) * 128]
             return carry
 
+        if k:
+            make_band(k)
         lax.fori_loop(0, per_seg // wide, body, 0)
         held = grid.at[own_slots(s)]
         copies = []
@@ -284,6 +294,18 @@
             total = total + far_r[k, i].astype(jnp.float32)
         out_ref[pl.ds(k * out_rows, out_rows), :] = total.astype(jnp.bfloat16)
 
+    make_band(0)
+    make_onehot()
+    raw_copy.wait()
+
+    @pl.when(t < tile_count - 1)
+    def _():
+        halo.wait_recv()
+
+    @pl.when(t == tile_count - 1)
+    def _():
+        raw_x[rim, :] = jnp.zeros((hop, raw_x.shape[1]), raw_x.dtype)
+
     gathers = {}
     arrivals = {}
     gathers[0] = envelope(0)
@@ -291,7 +313,6 @@
         if k + 1 < CHUNKS:
             gathers[k + 1] = envelope(k + 1)
         arrivals[k] = exchange(k, gathers[k])
-    make_onehot()
     sums = {}
     for k in range(CHUNKS):
         sums[k] = stack(k, arrivals[k])
@@ -326,18 +347,6 @@
     rings = seg_count // CORES
     depth = samples + hop
     bf16 = jnp.bfloat16
-    banded = jnp.stack(
-        [
-            jnp.pad(filters, ((0, 0), (hop * i, depth - taps - hop * i)))
-            for i in range(frames)
-        ],
-        1,
-    )
-    banded = (
-        banded.reshape(2, CHUNKS, fc, frames, depth)
-        .transpose(1, 0, 2, 3, 4)
-        .reshape(CHUNKS, 2 * rows, depth)
-    )
     dims = (seg_count, tile_count, hop, frames, per_seg, entries, steps, fc)
     other = max(rings - 1, 1)
     image = pl.pallas_call(
@@ -366,6 +375,7 @@
             pltpu.VMEM((CHUNKS, out_rows, part), bf16),
             pltpu.VMEM((CHUNKS, out_rows, part), jnp.float32),
             pltpu.VMEM((out_rows, part), jnp.float32),
+            pltpu.VMEM((2 * rows, depth), bf16),
             *[pltpu.VMEM((seg_count * per_seg, rows, 128), bf16) for _ in range(CHUNKS)],
             pltpu.SemaphoreType.DMA((1,)),
             pltpu.SemaphoreType.DMA((entries,)),
@@ -381,7 +391,7 @@
         compiler_params=pltpu.CompilerParams(
             collective_id=0, has_side_effects=True, vmem_limit_bytes=60 * 1024 * 1024
         ),
-    )(raw, banded, weights, blocks, shifts)
+    )(raw, filters, weights, blocks, shifts)
     return image.reshape(1, bank, steps, part)
 
 

time: 158 us -> 138 us (0.87)
  local copies, waits for them, and re-layouts: 13.9 us -> 3.14 us
  Pallas kernels: 143 us -> 135 us
    another operation x33 -> x0, local copies, waits for them, and re-layouts: 9.58 us -> none  [local(): jnp.stack([jnp.pad(filters, ((0, 0), (hop * i, depth - taps - hop * i)))...]
    pallas_call x1, Pallas kernels: 143 us -> 135 us  [local(): pl.pallas_call(functools.partial(kernel, dims), out_shape=jax.ShapeDtypeS...]
where the time goes in v2:
time: 138 us
  Pallas kernels  135 us (98%)
  local copies, waits for them, and re-layouts  3.14 us (2%)
    pallas_call x1, Pallas kernels, local(): pl.pallas_call(functools.partial(kernel, dims), out_shape=jax.ShapeDtypeS...  135 us
    unnamed x1, local copies, waits for them, and re-layouts  3.14 us

profile of v2, /device:TPU:16, one launch (start us, length us, event | category | flops | bytes accessed | tf_op | source)
XLA Modules:
  0.0 138.2 jit_solution(1619506496442402384)
XLA Ops:
  0.0 135.1 %shard_map.55 = bf16[1024,1024]{1,0:T(8,128)(2,1)} custom-call(bf16[1024,3072]{1,0:T(8,128)(2,1)} %raw_ref.1, bf16[32,128]{1,0:T(8,128)(2,1)} %taps_ref.1, bf16[1,8,4096,128]{3,2,1,0:T(8,128)(2,1)} %weights_ref.1, s32[8,32]{1,0:T(8,128)} %blocks_ref.1, s32[8,32]{1,0:T(8,128)} %shifts_ref.1), custom_call_target="tpu_custom_call" | custom-call | tf_op jit(solution)/shard_map/pallas_call | solution.py:352
  135.1 3.1 %copy.7 = bf16[1,16,64,1024]{3,2,1,0:T(8,128)(2,1)} copy(bf16[1,16,64,1024]{3,2,1,0:T(8,128)(2,1)} %bitcast.1) | data formatting | bytes 4194304

commit v3 on v2

--- a/solution.py
+++ b/solution.py
@@ -55,7 +55,14 @@
         return lax.rem(y + dy, rings) * CORES + core
 
     def peer_t(dt):
-        return lax.rem(t + dt, tile_count)
+        if tile_count & (tile_count - 1):
+            return lax.rem(t + dt, tile_count)
+        peer, weight = 0, 1
+        while weight < tile_count:
+            bit = (t // weight) % 2
+            peer = peer + weight * (1 - bit if dt & weight else bit)
+            weight *= 2
+        return peer
 
     raw_copy = pltpu.make_async_copy(raw_ref, raw_x.at[pl.ds(0, samples)], raw_sem.at[0])
     raw_copy.start()
@@ -104,7 +111,7 @@
         w_copies.append(copy)
 
     pending = []
-    wide = 2 if per_seg % 2 == 0 else 1
+    wide = next(w for w in (6, 4, 3, 2, 1) if per_seg % w == 0)
 
     def own_slots(seg):
         return pl.ds(seg * per_seg, per_seg)
@@ -175,7 +182,7 @@
 
         lax.fori_loop(0, tile_count, pick, 0)
         sent = []
-        order = sorted(range(1, tile_count), key=lambda dt: -min(dt, tile_count - dt))
+        order = sorted(range(1, tile_count), key=lambda dt: -dt)
         for dt in order:
             copy = remote(
                 picked.at[k, peer_t(dt)],

time: 138 us -> 140 us (1.014)
  the two profiles are of different devices: /device:TPU:16 before, /device:TPU:0 now
where the time goes in v3:
time: 140 us; the launch traced here: 139 us
  Pallas kernels  136 us (97%)
  local copies, waits for them, and re-layouts  3.14 us (2%)
    pallas_call x1, Pallas kernels, local(): pl.pallas_call(functools.partial(kernel, dims), out_shape=jax.ShapeDtypeS...  136 us
    unnamed x1, local copies, waits for them, and re-layouts  3.14 us

profile of v3, /device:TPU:0, one launch (start us, length us, event | category | flops | bytes accessed | tf_op | source)
XLA Modules:
  0.0 139.3 jit_solution(9792569547324710753)
XLA Ops:
  0.0 136.1 %shard_map.55 = bf16[1024,1024]{1,0:T(8,128)(2,1)} custom-call(bf16[1024,3072]{1,0:T(8,128)(2,1)} %raw_ref.1, bf16[32,128]{1,0:T(8,128)(2,1)} %taps_ref.1, bf16[1,8,4096,128]{3,2,1,0:T(8,128)(2,1)} %weights_ref.1, s32[8,32]{1,0:T(8,128)} %blocks_ref.1, s32[8,32]{1,0:T(8,128)} %shifts_ref.1), custom_call_target="tpu_custom_call" | custom-call | tf_op jit(solution)/shard_map/pallas_call | solution.py:359
  136.1 3.1 %copy.7 = bf16[1,16,64,1024]{3,2,1,0:T(8,128)(2,1)} copy(bf16[1,16,64,1024]{3,2,1,0:T(8,128)(2,1)} %bitcast.1) | data formatting | bytes 4194304
